TPU v7x, 32 devices: a whole 2x2x4 slice. The times are simulated.
32 devices in a mesh: tiles: 8 (over z, x), rep: 4 (over y, core).
Axes of the slice: x: 2, y: 2, z: 4, core: 2. Of those that a mesh axis runs over, the one named last changes fastest.
Arguments:
- affinity: bfloat16 [128, 512, 512], P(('tiles', 'rep')), may hold values from -0.25 to 0.25
- tile_pairs: int32 [128, 2], P(('tiles', 'rep')), may hold values from 0 to 31, as said below
- factors: float32 [32, 512, 256], P('tiles'), may hold values from -6 to 6
Outputs:
- polar_factors: float32 [32, 512, 256], P('tiles')
Inputs may be any that keep to these rules, and one draw needn't show every extreme that they name: `tile_pairs`: column 0 of a row is an image owned by the index of tiles that holds the row (images o * 4 to (o + 1) * 4 - 1 belong to index o); column 1 differs from column 0 by 1 to 4, and by exactly 4 in the first row held by every index of tiles.
All inputs are finite; a program needn't handle non-finite values.
Results may differ from a plain program's by a relative error of at most 0.0022.
Values may be sent and summed in bfloat16 or wider, within the bound.
A program may use at most 64 MiB of HBM per device.

v0:
```python
import math

import jax
import jax.numpy as jnp
from jax import lax
from jax.sharding import PartitionSpec as P

P_SIZE = 512
NS_STEPS = 6


epsilon = 1e-06
start_scale = 0.25
ascent_step = 0.25


def extended(block, sides, width):
    for axis, dim in sides:
        count = lax.axis_size(axis)
        forward = [(i, i + 1) for i in range(count - 1)]
        backward = [(target, source) for source, target in forward]
        low = lax.ppermute(
            lax.slice_in_dim(block, block.shape[dim] - width, None, axis=dim), axis, forward
        )
        high = lax.ppermute(lax.slice_in_dim(block, 0, width, axis=dim), axis, backward)
        block = jnp.concatenate([low, block, high], axis=dim)
    return block


def shifted(shard, axis, by):
    count = lax.axis_size(axis)
    pairs = [(i, i + by) for i in range(count) if 0 <= i + by < count]
    return lax.ppermute(shard, axis, pairs)


def polar_project(ascended):
    iterate = ascended
    for sweep_index in range(NS_STEPS):
        gram_matrix = jnp.einsum("npu,npv->nuv", iterate, iterate, precision=lax.Precision.HIGHEST)
        if sweep_index == 0:
            squares = jnp.trace(gram_matrix, axis1=1, axis2=2)[:, None, None]
            factor = start_scale * math.sqrt(iterate.shape[2]) * lax.rsqrt(squares + epsilon)
            iterate = iterate * factor
            gram_matrix = gram_matrix * (factor * factor)
        iterate = 1.5 * iterate - 0.5 * jnp.einsum(
            "npu,nuv->npv", iterate, gram_matrix, precision=lax.Precision.HIGHEST
        )
    return iterate * math.sqrt(P_SIZE)


def shards(affinity, tile_pairs, factors):
    per_owner = factors.shape[0]
    keypoints = factors.shape[1]
    universe = factors.shape[2]
    tile_count = affinity.shape[0]
    window_start = (lax.axis_index("tiles") - 1) * per_owner
    first_local = tile_pairs[:, 0] - window_start
    second_local = tile_pairs[:, 1] - window_start
    both_local = jnp.concatenate([first_local, second_local])
    window_slots = jnp.arange(3 * per_owner, dtype=jnp.int32)
    one_hot = (window_slots[:, None] == both_local[None, :]).astype(jnp.float32)
    image_count = per_owner // lax.axis_size("rep")
    image_start = lax.axis_index("rep") * image_count
    current = factors
    rounded = current.astype(jnp.bfloat16)
    window = extended(rounded, (("tiles", 0),), per_owner)
    first_rows = jnp.take(window, first_local, axis=0)
    second_rows = jnp.take(window, second_local, axis=0)
    forward = jnp.einsum("kab,kbu->kau", affinity, second_rows, preferred_element_type=jnp.float32)
    backward = jnp.einsum("kab,kau->kbu", affinity, first_rows, preferred_element_type=jnp.float32)
    tile_terms = jnp.concatenate([forward, backward]).reshape(2 * tile_count, keypoints * universe)
    window_sum = jnp.dot(one_hot, tile_terms, precision=lax.Precision.HIGHEST).reshape(
        3, per_owner, keypoints, universe
    )
    from_right = shifted(window_sum[0].astype(jnp.bfloat16), "tiles", -1).astype(jnp.float32)
    from_left = shifted(window_sum[2].astype(jnp.bfloat16), "tiles", 1).astype(jnp.float32)
    own_sum = window_sum[1] + from_right + from_left
    gradient = lax.psum_scatter(own_sum, "rep", scatter_dimension=0, tiled=True)
    own_images = lax.dynamic_slice_in_dim(current, image_start, image_count, 0)
    updated = polar_project(own_images + ascent_step * gradient)
    current = lax.all_gather(updated, "rep", axis=0, tiled=True)
    return current


def solution(mesh):
    in_specs = (P(("tiles", "rep"), None, None), P(("tiles", "rep"), None), P("tiles", None, None))
    out_specs = P("tiles", None, None)
    return jax.shard_map(shards, mesh=mesh, in_specs=in_specs, out_specs=out_specs, check_vma=False)
```

profile of v0, /device:TPU:3, one launch (start us, length us, event | category | flops | bytes accessed | tf_op | source)
XLA Modules:
  0.0 218.4 jit_solution(1634783378574034712)
XLA Ops:
  6.5 0.0 copy-start
  6.5 0.0 copy-start.1
  6.5 0.0 reduce-scatter.2.cloned.1.call-start
  6.5 1.9 convert_element_type.18
  8.4 1.9 collective-permute-start.1
  10.3 4.3 %collective-permute-start = (bf16[4,512,256]{2,1,0:T(8,128)(2,1)S(1)}, bf16[4,512,256]{2,1,0:T(8,128)(2,1)}, u32[]{:S(2)}, u32[]{:S(2)}) collective-permute-start(bf16[4,512,256]{2,1,0:T(8,128)(2,1)S(1)} %convert_element_type.18), channel_id=1, source_target_pairs={{0,4},{4,8},{8,12},{12,16},{16,20},{20,24},{24,28},{1,5},{5,9},{9,... | collective-permute-start | bytes 3145736 | tf_op jit(solution)/shard_map/ppermute | solution.py:22
  14.6 0.0 copy-done.1
  14.6 0.1 pad_add_fusion
  14.7 20.6 %collective-permute-done.1 = bf16[4,512,256]{2,1,0:T(8,128)(2,1)} collective-permute-done((bf16[4,512,256]{2,1,0:T(8,128)(2,1)S(1)}, bf16[4,512,256]{2,1,0:T(8,128)(2,1)}, u32[]{:S(2)}, u32[]{:S(2)}) %collective-permute-start.1) | collective-permute-done | bytes 1048608 | tf_op jit(solution)/shard_map/ppermute | solution.py:25
  35.4 23.5 %collective-permute-done = bf16[4,512,256]{2,1,0:T(8,128)(2,1)} collective-permute-done((bf16[4,512,256]{2,1,0:T(8,128)(2,1)S(1)}, bf16[4,512,256]{2,1,0:T(8,128)(2,1)}, u32[]{:S(2)}, u32[]{:S(2)}) %collective-permute-start) | collective-permute-done | bytes 1048608 | tf_op jit(solution)/shard_map/ppermute | solution.py:22
  58.9 3.0 %pad_maximum_fusion.1 = bf16[12,512,256]{2,1,0:T(8,128)(2,1)} fusion(bf16[4,512,256]{2,1,0:T(8,128)(2,1)} %collective-permute-done.1, bf16[4,512,256]{2,1,0:T(8,128)(2,1)S(1)} %convert_element_type.18, bf16[4,512,256]{2,1,0:T(8,128)(2,1)} %collective-permute-done), kind=kLoop, calls=%fused_computation.3 | loop fusion | flops 3145728 | bytes 6291456 | tf_op jit(solution)/shard_map/concatenate | solution.py:26
  61.9 2.5 %gather_fusion.1 = bf16[4,512,256]{2,1,0:T(8,128)(2,1)S(1)} fusion(bf16[12,512,256]{2,1,0:T(8,128)(2,1)} %pad_maximum_fusion.1, s32[1024]{0:T(1024)S(1)} %pad_clamp_fusion), kind=kCustom, calls=%fused_computation.1.clone | custom fusion | bytes 2097168 | tf_op jit(solution)/shard_map/jit(_take)/gather | solution.py:67
  64.4 3.5 %gather_fusion = bf16[4,512,256]{2,1,0:T(8,128)(2,1)} fusion(bf16[12,512,256]{2,1,0:T(8,128)(2,1)} %pad_maximum_fusion.1, s32[1024]{0:T(1024)S(1)} %pad_clamp_fusion.1), kind=kCustom, calls=%fused_computation.clone | custom fusion | bytes 2097168 | tf_op jit(solution)/shard_map/jit(_take)/gather | solution.py:68
  67.9 0.0 copy-done
  67.9 2.1 convolution_bitcast_fusion.1
  70.0 0.8 convolution_bitcast_fusion
  70.8 2.4 %pad_maximum_fusion = f32[8,512,256]{1,2,0:T(8,128)} fusion(f32[4,512,256]{1,2,0:T(8,128)S(1)} %convolution_bitcast_fusion, f32[4,512,256]{1,2,0:T(8,128)S(1)} %convolution_bitcast_fusion.1), kind=kLoop, calls=%fused_computation.2 | loop fusion | flops 1048576 | bytes 8388608 | tf_op jit(solution)/shard_map/concatenate | solution.py:71
  73.2 5.4 %copy.11 = f32[8,512,256]{2,1,0:T(8,128)} copy(f32[8,512,256]{1,2,0:T(8,128)} %pad_maximum_fusion) | data formatting | bytes 8388608 | tf_op jit(solution)/shard_map/concatenate | solution.py:71
  78.6 4.6 %copy.14 = f32[1,8,512,256]{3,1,2,0:T(8,128)S(1)} copy(f32[1,8,512,256]{3,2,1,0:T(8,128)} %bitcast.93) | data formatting | bytes 8388608
  83.2 3.5 %fusion.51 = (bf16[12,131072]{1,0:T(8,128)(2,1)S(1)}, f32[12,131072]{1,0:T(8,128)S(1)}) fusion(f32[8,131072]{1,0:T(8,128)S(1)} %bitcast.92, s32[8]{0:T(128)S(1)} %pad_add_fusion), kind=kOutput, calls=%fused_computation.79 | convolution fusion | flops 152567904 | bytes 13631520 | tf_op jit(solution)/shard_map/dot_general | solution.py:72
  86.7 0.5 fusion.50
  87.2 0.1 copy.22
  87.4 0.1 copy.21
  87.5 2.1 collective-permute-start.3
  89.6 3.3 %collective-permute-start.2 = (bf16[4,512,256]{2,1,0:T(8,128)(2,1)S(1)}, bf16[4,512,256]{2,1,0:T(8,128)(2,1)S(1)}, u32[]{:S(2)}, u32[]{:S(2)}) collective-permute-start(bf16[4,512,256]{2,1,0:T(8,128)(2,1)S(1)} %bitcast.97), channel_id=1, source_target_pairs={{4,0},{8,4},{12,8},{16,12},{20,16},{24,20},{28,24},{5,1},{9,5},{13... | collective-permute-start | bytes 3145736 | tf_op jit(solution)/shard_map/ppermute | solution.py:33
  92.9 0.5 slice.29
  93.3 42.8 %collective-permute-done.3 = bf16[4,512,256]{2,1,0:T(8,128)(2,1)S(1)} collective-permute-done((bf16[4,512,256]{2,1,0:T(8,128)(2,1)S(1)}, bf16[4,512,256]{2,1,0:T(8,128)(2,1)S(1)}, u32[]{:S(2)}, u32[]{:S(2)}) %collective-permute-start.3) | collective-permute-done | bytes 1048608 | tf_op jit(solution)/shard_map/ppermute | solution.py:33
  136.1 0.0 collective-permute-done.2
  136.1 1.8 fusion
  137.9 0.0 reduce-scatter.2.cloned.1.call-update
  137.9 0.2 all-gather.2.cloned.1.call-start
  138.2 32.2 %reduce-scatter.2.cloned.1.call-done = f32[1,512,256]{2,1,0:T(8,128)} async-done(((f32[4,512,256]{2,1,0:T(8,128)}), f32[1,512,256]{2,1,0:T(8,128)}) %reduce-scatter.2.cloned.1.call-update) | async-done | bytes 524304 | tf_op jit(solution)/shard_map/reduce_scatter | solution.py:78
  170.4 3.1 %select_reduce_fusion = (f32[]{:T(128)}, f32[256,256]{1,0:T(8,128)S(1)}) fusion(f32[1,512,256]{2,1,0:T(8,128)} %reduce-scatter.2.cloned.1.call-done, f32[4,512,256]{2,1,0:T(8,128)} %param.7, s32[]{:T(128)S(6)} %select_n.16), kind=kOutput, calls=%fused_computation.57 | convolution fusion | flops 403111936 | bytes 1310728 | tf_op jit(solution)/shard_map/npu,npv->nuv/dot_general | solution.py:39
  174.2 2.2 fusion.7
  176.4 1.0 fusion.31
  177.4 0.6 fusion.8
  178.0 1.0 fusion.28
  179.0 0.6 fusion.9
  179.6 1.0 fusion.25
  180.7 0.6 fusion.10
  181.3 1.0 fusion.22
  182.3 0.6 fusion.11
  182.9 1.0 fusion.19
  184.0 1.4 fusion.13
  185.3 0.0 all-gather.2.cloned.1.call-update
  185.4 23.1 %all-gather.2.cloned.1.call-done = f32[4,512,256]{2,1,0:T(8,128)} async-done(((f32[1,512,256]{2,1,0:T(8,128)}), f32[4,512,256]{2,1,0:T(8,128)}) %all-gather.2.cloned.1.call-update) | async-done | bytes 2097168 | tf_op jit(solution)/shard_map/all_gather | solution.py:81
  208.5 3.0 %copy.24 = f32[4,512,256]{2,1,0:T(8,128)} copy(f32[4,512,256]{2,1,0:T(8,128)} %all-gather.2.cloned.1.call-done) | data formatting | bytes 4194304
  (4 shorter events, 0.0 us)
Async XLA Ops:
  6.5 61.3 %copy-start = (bf16[4,512,512]{2,1,0:T(8,128)(2,1)S(1)}, bf16[4,512,512]{2,1,0:T(8,128)(2,1)}, u32[]{:S(2)}) copy-start(bf16[4,512,512]{2,1,0:T(8,128)(2,1)} %param.5) | copy-start | bytes 6291460
  6.5 8.1 %copy-start.1 = (s32[4,2]{0,1:T(2,128)S(1)}, s32[4,2]{0,1:T(2,128)}, u32[]{:S(2)}) copy-start(s32[4,2]{0,1:T(2,128)} %param.6) | copy-start | bytes 100
  6.5 163.8 %reduce-scatter.2.cloned.1.call-start = ((), (), s32[]{:S(2)}) async-start(), calls=%async_computation.1 | async-start | bytes 2621440 | tf_op jit(solution)/shard_map/reduce_scatter | solution.py:78
  8.4 27.0 %collective-permute-start.1 = (bf16[4,512,256]{2,1,0:T(8,128)(2,1)S(1)}, bf16[4,512,256]{2,1,0:T(8,128)(2,1)}, u32[]{:S(2)}, u32[]{:S(2)}) collective-permute-start(bf16[4,512,256]{2,1,0:T(8,128)(2,1)S(1)} %convert_element_type.18), channel_id=1, source_target_pairs={{4,0},{8,4},{12,8},{16,12},{20,16},{24,20},{28,24},{5,1},{9,5},{13... | collective-permute-start | bytes 3145736 | tf_op jit(solution)/shard_map/ppermute | solution.py:25
  10.3 48.5 %collective-permute-start = (bf16[4,512,256]{2,1,0:T(8,128)(2,1)S(1)}, bf16[4,512,256]{2,1,0:T(8,128)(2,1)}, u32[]{:S(2)}, u32[]{:S(2)}) collective-permute-start(bf16[4,512,256]{2,1,0:T(8,128)(2,1)S(1)} %convert_element_type.18), channel_id=1, source_target_pairs={{0,4},{4,8},{8,12},{12,16},{16,20},{20,24},{24,28},{1,5},{5,9},{9,... | collective-permute-start | bytes 3145736 | tf_op jit(solution)/shard_map/ppermute | solution.py:22
  87.5 48.6 %collective-permute-start.3 = (bf16[4,512,256]{2,1,0:T(8,128)(2,1)S(1)}, bf16[4,512,256]{2,1,0:T(8,128)(2,1)S(1)}, u32[]{:S(2)}, u32[]{:S(2)}) collective-permute-start(bf16[4,512,256]{2,1,0:T(8,128)(2,1)S(1)} %bitcast.98), channel_id=1, source_target_pairs={{0,4},{4,8},{8,12},{12,16},{16,20},{20,24},{24,28},{1,5},{5,9},{9,... | collective-permute-start | bytes 3145736 | tf_op jit(solution)/shard_map/ppermute | solution.py:33
  89.6 46.5 %collective-permute-start.2 = (bf16[4,512,256]{2,1,0:T(8,128)(2,1)S(1)}, bf16[4,512,256]{2,1,0:T(8,128)(2,1)S(1)}, u32[]{:S(2)}, u32[]{:S(2)}) collective-permute-start(bf16[4,512,256]{2,1,0:T(8,128)(2,1)S(1)} %bitcast.97), channel_id=1, source_target_pairs={{4,0},{8,4},{12,8},{16,12},{20,16},{24,20},{28,24},{5,1},{9,5},{13... | collective-permute-start | bytes 3145736 | tf_op jit(solution)/shard_map/ppermute | solution.py:33
  137.9 70.6 %all-gather.2.cloned.1.call-start = ((), (), s32[]{:S(2)}) async-start(), calls=%async_computation.2 | async-start | bytes 2621440 | tf_op jit(solution)/shard_map/all_gather | solution.py:81
Sparse Core Ops, SparseCore 0:
  138.1 32.2 reduce-scatter.1
  185.5 22.9 all-gather.1
where the time goes:
time: 220 us; the launch traced here: 218 us
  waiting for transfers between devices  142 us (65%)
  matrix products  20.6 us (9%)
  local copies, waits for them, and re-layouts  20.3 us (9%)
  between operations  14.3 us (6%)
  starting transfers between devices  11.8 us (5%)
  other arithmetic  9.18 us (4%)
    ppermute x2, waiting for transfers between devices, shifted(): return lax.ppermute(shard, axis, pairs)  42.8 us
    reduce_scatter x1, waiting for transfers between devices, shards(): gradient = lax.psum_scatter(own_sum, 'rep', scatter_dimension=0, tiled=True)  32.2 us
    ppermute x1, waiting for transfers between devices, extended(): lax.ppermute(lax.slice_in_dim(block, block.shape[dim] - width, None, axis...  23.5 us
    all_gather x1, waiting for transfers between devices, shards(): current = lax.all_gather(updated, 'rep', axis=0, tiled=True)  23.1 us
    ppermute x1, waiting for transfers between devices, extended(): lax.ppermute(lax.slice_in_dim(block, 0, width, axis=dim), axis, backward)  20.6 us
    dot_general x6, matrix products, polar_project(): jnp.einsum('npu,npv->nuv', iterate, iterate, precision=lax.Precision.HIGH...  8.32 us
    unnamed x8, local copies, waits for them, and re-layouts  7.95 us
    dot_general x6, matrix products, polar_project(): jnp.einsum('npu,nuv->npv', iterate, gram_matrix, precision=lax.Precision....  5.87 us
  transfers between devices with their start and end apart: 6, of which 5 were waited for; matrix products, arithmetic and copies ran while one was open for 0% of the time, Pallas kernels for 0%

commit v1 on v0

v1 whole, which is shorter than its diff:
```python
import functools
import math

import jax
import jax.numpy as jnp
from jax import lax
from jax.experimental import pallas as pl
from jax.experimental.pallas import tpu as pltpu
from jax.sharding import PartitionSpec as P

NS_STEPS = 6

epsilon = 1e-06
start_scale = 0.25
ascent_step = 0.25

CHUNKS = 2
LEFT, RIGHT, OWN = 0, 1, 2


def dot(a, b):
    return jnp.dot(a, b, preferred_element_type=jnp.float32)


def dot_t(a, b):
    return lax.dot_general(a, b, (((0,), (0,)), ((), ())), preferred_element_type=jnp.float32)


def split(x):
    high = x.astype(jnp.bfloat16)
    return high, (x - high.astype(jnp.float32)).astype(jnp.bfloat16)


def dot3(a, b):
    return dot(a[0], b[0]) + (dot(a[0], b[1]) + dot(a[1], b[0]))


def kernel(
    owners, rep, pairs_ref, aff_hbm, fac_hbm, out_ref, own_ref,
    aff, fac, held, win, back, forw, s1, r1, s2, r2, s3, r3, asc,
    load_sem, wx_s, wx_r, wy_s, wy_r, wc_s, wc_r,
    g1_s, g1_r, g2_s, g2_r, g3_s, g3_r, oy_s, oy_r, oc_s, oc_r,
):
    count, keypoints, universe = fac.shape
    tiles = aff.shape[0]
    pairs = rep // 2
    t = lax.axis_index("tiles")
    r = lax.axis_index("rep")
    p, c = r // 2, r % 2
    sibling = {"rep": 2 * p + (1 - c)}
    has = (t > 0, t < owners - 1)
    towards = ({"tiles": t - 1}, {"tiles": t + 1})
    rows_of = [
        pl.ds(i * (keypoints // CHUNKS), keypoints // CHUNKS) for i in range(CHUNKS)
    ]
    sent = []

    def pair_at(d):
        return lax.rem(p + d, pairs)

    def across(d):
        return {"rep": 2 * pair_at(d) + c}

    def send(src, dst, ssem, rsem, device, when=None):
        copy = pltpu.make_async_remote_copy(
            src_ref=src, dst_ref=dst, send_sem=ssem, recv_sem=rsem,
            device_id=device, device_id_type=pl.DeviceIdType.MESH,
        )
        if when is None:
            copy.start()
        else:
            pl.when(when)(lambda: copy.start())
        sent.append((copy, when))

    def arrived(dst, ssem, rsem, device):
        pltpu.make_async_remote_copy(
            src_ref=dst, dst_ref=dst, send_sem=ssem, recv_sem=rsem,
            device_id=device, device_id_type=pl.DeviceIdType.MESH,
        ).wait_recv()

    def fac_load(i, sem):
        return pltpu.make_async_copy(fac_hbm.at[i], fac.at[i], load_sem.at[sem])

    aff_loads = [
        pltpu.make_async_copy(aff_hbm.at[k], aff.at[k], load_sem.at[count + k])
        for k in range(tiles)
    ]
    order = [lax.rem(r + i, count) for i in range(count)]
    fac_loads = [fac_load(order[i], i) for i in range(count)]
    for copy in fac_loads:
        copy.start()
    for copy in aff_loads:
        copy.start()

    barrier = pltpu.get_barrier_semaphore()
    for side in (LEFT, RIGHT):
        @pl.when(has[side])
        def _():
            pl.semaphore_signal(
                barrier, inc=1, device_id=towards[side], device_id_type=pl.DeviceIdType.MESH
            )
    pl.semaphore_signal(barrier, inc=1, device_id=sibling, device_id_type=pl.DeviceIdType.MESH)
    for d in range(1, pairs):
        pl.semaphore_signal(
            barrier, inc=1, device_id=across(d), device_id_type=pl.DeviceIdType.MESH
        )

    def convert(i):
        fac_loads[i].wait()
        block = fac[order[i]].astype(jnp.bfloat16)
        held[order[i]] = block
        win[count + order[i]] = block

    convert(0)
    neighbours = jnp.where(has[LEFT], 1, 0) + jnp.where(has[RIGHT], 1, 0)
    pl.semaphore_wait(barrier, pairs + neighbours)

    for h, rows in enumerate(rows_of):
        for side in (LEFT, RIGHT):
            there = 1 - side
            send(
                held.at[r, rows], win.at[2 * count * there + r, rows],
                wx_s.at[side, h], wx_r.at[there, h], towards[side], has[side],
            )
    for side in (LEFT, RIGHT):
        @pl.when(jnp.logical_not(has[side]))
        def _():
            win[pl.ds(2 * count * side, count)] = jnp.zeros(
                (count, keypoints, universe), jnp.bfloat16
            )
            r3[side] = jnp.zeros((keypoints, universe), jnp.bfloat16)

    for i in range(1, count):
        convert(i)

    first = [pairs_ref[k, 0] - t * count for k in range(tiles)]
    second = [pairs_ref[k, 1] - (t - 1) * count for k in range(tiles)]
    for k in range(tiles):
        aff_loads[k].wait()
        back[k] = dot_t(aff[k], held[jnp.clip(first[k], 0, count - 1)])

    def partial(side, m, rows):
        slot = (0, 2 * count, count)[side] + m
        total = jnp.where(second[0] == slot, 1.0, 0.0) * back[0, rows]
        for k in range(1, tiles):
            total += jnp.where(second[k] == slot, 1.0, 0.0) * back[k, rows]
        if side == OWN:
            for k in range(tiles):
                total += jnp.where(first[k] == m, 1.0, 0.0) * forw[k, rows]
        return total

    def pair_send(side, h):
        rows = rows_of[h]
        for q in range(pairs):
            s1[side, h, q] = partial(side, 2 * q + (1 - c), rows).astype(jnp.bfloat16)
        send(
            s1.at[side, h], r1.at[side, h], g1_s.at[side, h], g1_r.at[side, h], sibling
        )

    def across_send(side, h):
        rows = rows_of[h]
        arrived(r1.at[side, h], g1_s.at[side, h], g1_r.at[side, h], sibling)
        for d in range(1, pairs):
            q = pair_at(d)
            s2[side, h, d - 1] = (
                partial(side, 2 * q + c, rows) + r1[side, h, q].astype(jnp.float32)
            ).astype(jnp.bfloat16)
            send(
                s2.at[side, h, d - 1], r2.at[side, h, d - 1],
                g2_s.at[side, h, d - 1], g2_r.at[side, h, d - 1], across(d),
            )

    def rep_sum(side, h):
        rows = rows_of[h]
        total = partial(side, r, rows) + r1[side, h, p].astype(jnp.float32)
        for d in range(1, pairs):
            arrived(
                r2.at[side, h, d - 1], g2_s.at[side, h, d - 1], g2_r.at[side, h, d - 1], across(d)
            )
            total += r2[side, h, d - 1].astype(jnp.float32)
        return total

    def window_slot(side, m, rows):
        return win.at[2 * count * side + m, rows]

    def window_out(h):
        rows = rows_of[h]
        for side in (LEFT, RIGHT):
            mine = window_slot(side, r, rows)

            @pl.when(has[side])
            def _():
                arrived(mine, wx_s.at[side, h], wx_r.at[side, h], towards[side])

            for d in range(1, pairs):
                send(
                    mine, mine, wy_s.at[side, h, d - 1], wy_r.at[side, h, d - 1],
                    across(d), has[side],
                )
            send(mine, mine, wc_s.at[side, h, 0], wc_r.at[side, h, 0], sibling, has[side])

    def window_pass(h):
        rows = rows_of[h]
        for side in (LEFT, RIGHT):
            for d in range(1, pairs):
                q = lax.rem(p - d + pairs, pairs)
                theirs = window_slot(side, 2 * q + c, rows)

                @pl.when(has[side])
                def _():
                    arrived(
                        theirs, wy_s.at[side, h, d - 1], wy_r.at[side, h, d - 1], across(d)
                    )

                send(
                    theirs, theirs, wc_s.at[side, h, d], wc_r.at[side, h, d], sibling, has[side]
                )

    def window_end(h):
        rows = rows_of[h]
        for side in (LEFT, RIGHT):
            for d in range(pairs):
                q = lax.rem(p - d + pairs, pairs)

                @pl.when(has[side])
                def _():
                    arrived(
                        window_slot(side, 2 * q + (1 - c), rows),
                        wc_s.at[side, h, d], wc_r.at[side, h, d], sibling,
                    )

    for h in range(CHUNKS):
        for side in (LEFT, RIGHT):
            pair_send(side, h)
    for h in range(CHUNKS):
        window_out(h)
        for side in (LEFT, RIGHT):
            across_send(side, h)
    for h in range(CHUNKS):
        window_pass(h)
        for side in (LEFT, RIGHT):
            s3[side, rows_of[h]] = rep_sum(side, h).astype(jnp.bfloat16)
            send(
                s3.at[side, rows_of[h]], r3.at[1 - side, rows_of[h]],
                g3_s.at[side, h], g3_r.at[1 - side, h], towards[side], has[side],
            )
    for h in range(CHUNKS):
        window_end(h)

    for h, rows in enumerate(rows_of):
        for k in range(tiles):
            forw[k, rows] = dot(aff[k, rows], win[jnp.clip(second[k], 0, 3 * count - 1)])
        pair_send(OWN, h)
    for h in range(CHUNKS):
        across_send(OWN, h)
    gram = None
    squares = None
    parts = []
    for h, rows in enumerate(rows_of):
        total = rep_sum(OWN, h)
        for side in (LEFT, RIGHT):
            @pl.when(has[side])
            def _():
                arrived(
                    r3.at[side, rows], g3_s.at[side, h], g3_r.at[side, h], towards[side]
                )
            total += r3[side, rows].astype(jnp.float32)
        ascended = fac[r, rows] + ascent_step * total
        asc[rows] = ascended
        high, low = split(ascended)
        cross = dot_t(high, low)
        part = dot_t(high, high) + (cross + cross.T)
        gram = part if gram is None else gram + part
        ss = jnp.sum(ascended * ascended)
        squares = ss if squares is None else squares + ss

    factor = start_scale * math.sqrt(universe) * lax.rsqrt(
        jnp.full((1, 1), squares, jnp.float32) + epsilon
    )
    gram = gram * (factor * factor)
    eye = (
        lax.broadcasted_iota(jnp.int32, (universe, universe), 0)
        == lax.broadcasted_iota(jnp.int32, (universe, universe), 1)
    ).astype(jnp.float32)
    product = None
    for step in range(NS_STEPS):
        mix = split(1.5 * eye - 0.5 * gram)
        if product is None:
            product = 1.5 * eye - 0.5 * gram
        else:
            product = dot3(split(product), mix)
        if step < NS_STEPS - 1:
            gram = dot3(split(dot3(split(gram), mix)), mix)
    product = split(product * (factor * math.sqrt(keypoints)))

    for h, rows in enumerate(rows_of):
        result = dot3(split(asc[rows]), product)
        own_ref[rows] = result
        out_ref[r, rows] = result.astype(jnp.bfloat16)
        mine = out_ref.at[r, rows]
        for d in range(1, pairs):
            send(mine, mine, oy_s.at[h, d - 1], oy_r.at[h, d - 1], across(d))
        send(mine, mine, oc_s.at[h, 0], oc_r.at[h, 0], sibling)
    for h, rows in enumerate(rows_of):
        for d in range(1, pairs):
            q = lax.rem(p - d + pairs, pairs)
            theirs = out_ref.at[2 * q + c, rows]
            arrived(theirs, oy_s.at[h, d - 1], oy_r.at[h, d - 1], across(d))
            send(theirs, theirs, oc_s.at[h, d], oc_r.at[h, d], sibling)
    for h, rows in enumerate(rows_of):
        for d in range(pairs):
            q = lax.rem(p - d + pairs, pairs)
            arrived(
                out_ref.at[2 * q + (1 - c), rows], oc_s.at[h, d], oc_r.at[h, d], sibling
            )
    for copy, when in sent:
        if when is None:
            copy.wait_send()
        else:
            pl.when(when)(lambda: copy.wait_send())


def shards(owners, rep, affinity, tile_pairs, factors):
    count, keypoints, universe = factors.shape
    tiles = affinity.shape[0]
    assert count == rep and rep % 2 == 0
    pairs = rep // 2
    half = keypoints // CHUNKS
    bf, f32 = jnp.bfloat16, jnp.float32
    image = (keypoints, universe)
    dma = pltpu.SemaphoreType.DMA
    C = CHUNKS
    D = max(pairs - 1, 1)
    gathered, own = pl.pallas_call(
        functools.partial(kernel, owners, rep),
        out_shape=(
            jax.ShapeDtypeStruct((count, *image), bf),
            jax.ShapeDtypeStruct(image, f32),
        ),
        in_specs=[
            pl.BlockSpec(memory_space=pltpu.SMEM),
            pl.BlockSpec(memory_space=pl.ANY),
            pl.BlockSpec(memory_space=pl.ANY),
        ],
        out_specs=(
            pl.BlockSpec(memory_space=pltpu.VMEM),
            pl.BlockSpec(memory_space=pltpu.VMEM),
        ),
        scratch_shapes=[
            pltpu.VMEM(affinity.shape, bf),
            pltpu.VMEM(factors.shape, f32),
            pltpu.VMEM(factors.shape, bf),
            pltpu.VMEM((3 * count, *image), bf),
            pltpu.VMEM((tiles, *image), f32),
            pltpu.VMEM((tiles, *image), f32),
            pltpu.VMEM((3, C, pairs, half, universe), bf),
            pltpu.VMEM((3, C, pairs, half, universe), bf),
            pltpu.VMEM((3, C, D, half, universe), bf),
            pltpu.VMEM((3, C, D, half, universe), bf),
            pltpu.VMEM((2, *image), bf),
            pltpu.VMEM((2, *image), bf),
            pltpu.VMEM(image, f32),
            dma((count + tiles,)),
            dma((2, C)), dma((2, C)),
            dma((2, C, D)), dma((2, C, D)),
            dma((2, C, pairs)), dma((2, C, pairs)),
            dma((3, C)), dma((3, C)),
            dma((3, C, D)), dma((3, C, D)),
            dma((2, C)), dma((2, C)),
            dma((C, D)), dma((C, D)),
            dma((C, pairs)), dma((C, pairs)),
        ],
        compiler_params=pltpu.CompilerParams(
            collective_id=0, has_side_effects=True, vmem_limit_bytes=48 * 1024 * 1024
        ),
    )(tile_pairs, affinity, factors)
    mine = lax.broadcasted_iota(jnp.int32, (count, 1, 1), 0) == lax.axis_index("rep")
    return jnp.where(mine, own[None], gathered.astype(f32))


def solution(mesh):
    in_specs = (P(("tiles", "rep"), None, None), P(("tiles", "rep"), None), P("tiles", None, None))
    out_specs = P("tiles", None, None)
    body = functools.partial(shards, mesh.shape["tiles"], mesh.shape["rep"])
    return jax.shard_map(body, mesh=mesh, in_specs=in_specs, out_specs=out_specs, check_vma=False)
```

time: 220 us -> 64.3 us (0.29)
  waiting for transfers between devices: 142 us -> 0 us
  Pallas kernels: 0 us -> 58.5 us
  matrix products: 20.6 us -> 0 us
  local copies, waits for them, and re-layouts: 20.3 us -> 3.95 us
  between operations: 14.3 us -> 0.01 us
  starting transfers between devices: 11.8 us -> 0 us
  other arithmetic: 9.18 us -> 1.58 us
    ppermute x4 -> x0, waiting for transfers between devices: 86.9 us -> none  [the longest x2 42.8 us: shifted(): return lax.ppermute(shard, axis, pairs)]
    pallas_call x0 -> x1, Pallas kernels: none -> 58.5 us  [shards(): pl.pallas_call(functools.partial(kernel, owners, rep), out_shape=(jax.Sha...]
    reduce_scatter x1 -> x0, waiting for transfers between devices: 32.2 us -> none  [shards(): gradient = lax.psum_scatter(own_sum, 'rep', scatter_dimension=0, tiled=True)]
    all_gather x1 -> x0, waiting for transfers between devices: 23.1 us -> none  [shards(): current = lax.all_gather(updated, 'rep', axis=0, tiled=True)]
    dot_general x15 -> x0, matrix products: 20.6 us -> none  [the longest x6 8.32 us: polar_project(): jnp.einsum('npu,npv->nuv', iterate, iterate, precision=lax.Precision.HIGH...]
    ppermute x4 -> x0, starting transfers between devices: 11.5 us -> none  [the longest x2 5.34 us: shifted(): return lax.ppermute(shard, axis, pairs)]
    gather x2 -> x0, local copies, waits for them, and re-layouts: 5.97 us -> none  [the longest x1 3.47 us: shards(): second_rows = jnp.take(window, second_local, axis=0)]
    concatenate x3 -> x0, other arithmetic: 5.49 us -> none  [the longest x1 3.02 us: extended(): block = jnp.concatenate([low, block, high], axis=dim)]
  transfers between devices with their start and end apart: 6 -> 0, of which waited for: 5 -> 0; matrix products, arithmetic and copies ran while one was open for 0% -> 0% of each run, Pallas kernels for 0% -> 0%
where the time goes in v1:
time: 64.3 us; the launch traced here: 64.1 us
  Pallas kernels  58.5 us (91%)
  local copies, waits for them, and re-layouts  3.95 us (6%)
  other arithmetic  1.58 us (2%)
    pallas_call x1, Pallas kernels, shards(): pl.pallas_call(functools.partial(kernel, owners, rep), out_shape=(jax.Sha...  58.5 us
    unnamed x5, local copies, waits for them, and re-layouts  3.95 us
    select_n x1, other arithmetic, shards(): return jnp.where(mine, own[None], gathered.astype(f32))  1.58 us

profile of v1, /device:TPU:3, one launch (start us, length us, event | category | flops | bytes accessed | tf_op | source)
XLA Modules:
  0.0 64.1 jit_solution(3169407525311359080)
XLA Ops:
  0.0 0.8 %copy.4.pairs_ref = s32[4,2]{1,0:T(4,128)S(1)} copy(s32[4,2]{0,1:T(2,128)} %param.4) | data formatting | bytes 64 | tf_op args[1]
  0.8 0.0 copy-start
  0.8 1.6 %copy-done = bf16[4,512,512]{2,1,0:T(8,128)(2,1)S(1)} copy-done((bf16[4,512,512]{2,1,0:T(8,128)(2,1)S(1)}, bf16[4,512,512]{2,1,0:T(8,128)(2,1)}, u32[]{:S(2)}) %copy-start) | copy-done | bytes 2097176
  2.4 0.0 copy-start.1
  2.4 1.6 %copy-done.1 = f32[4,512,256]{2,1,0:T(8,128)S(1)} copy-done((f32[4,512,256]{2,1,0:T(8,128)S(1)}, f32[4,512,256]{2,1,0:T(8,128)}, u32[]{:S(2)}) %copy-start.1) | copy-done | bytes 2097176
  4.0 58.5 %shard_map.37 = (bf16[4,512,256]{2,1,0:T(8,128)(2,1)S(1)}, f32[512,256]{1,0:T(8,128)S(1)}) custom-call(s32[4,2]{1,0:T(4,128)S(1)} %copy.4.pairs_ref, bf16[4,512,512]{2,1,0:T(8,128)(2,1)S(1)} %copy-done, f32[4,512,256]{2,1,0:T(8,128)S(1)} %copy-done.1), custom_call_target="tpu_custom_call" | custom-call | tf_op jit(solution)/shard_map/pallas_call | solution.py:334
  62.5 1.6 %convert_select_fusion = f32[4,512,256]{2,1,0:T(8,128)} fusion(bf16[4,512,256]{2,1,0:T(8,128)(2,1)S(1)} %get-tuple-element.8, f32[512,256]{1,0:T(8,128)S(1)} %get-tuple-element.7, pred[4]{0:T(512)(128)(4,1)S(1)} %iota_compare_fusion), kind=kLoop, calls=%fused_computation | loop fusion | flops 1048576 | bytes 3670020 | tf_op jit(solution)/shard_map/jit(_where)/select_n | solution.py:378
  (1 shorter events, 0.0 us)
Async XLA Ops:
  0.8 1.6 %copy-start = (bf16[4,512,512]{2,1,0:T(8,128)(2,1)S(1)}, bf16[4,512,512]{2,1,0:T(8,128)(2,1)}, u32[]{:S(2)}) copy-start(bf16[4,512,512]{2,1,0:T(8,128)(2,1)} %aff_hbm.1) | copy-start | bytes 6291460
  2.4 1.6 %copy-start.1 = (f32[4,512,256]{2,1,0:T(8,128)S(1)}, f32[4,512,256]{2,1,0:T(8,128)}, u32[]{:S(2)}) copy-start(f32[4,512,256]{2,1,0:T(8,128)} %fac_hbm.1) | copy-start | bytes 6291460

commit v2 on v1

--- a/solution.py
+++ b/solution.py
@@ -50,6 +50,11 @@
     sibling = {"rep": 2 * p + (1 - c)}
     has = (t > 0, t < owners - 1)
     towards = ({"tiles": t - 1}, {"tiles": t + 1})
+    odd = lax.rem(t, 2)
+    near, onward = t + 1 - 2 * odd, 2 - 4 * odd
+    near_base, far_base = 2 * count * (1 - odd), 2 * count * odd
+    passes = (t + onward >= 0) & (t + onward < owners)
+    fed = (t - onward >= 0) & (t - onward < owners)
     rows_of = [
         pl.ds(i * (keypoints // CHUNKS), keypoints // CHUNKS) for i in range(CHUNKS)
     ]
@@ -85,7 +90,7 @@
         pltpu.make_async_copy(aff_hbm.at[k], aff.at[k], load_sem.at[count + k])
         for k in range(tiles)
     ]
-    order = [lax.rem(r + i, count) for i in range(count)]
+    order = [2 * q + c for q in range(pairs)] + [2 * q + (1 - c) for q in range(pairs)]
     fac_loads = [fac_load(order[i], i) for i in range(count)]
     for copy in fac_loads:
         copy.start()
@@ -93,11 +98,15 @@
         copy.start()
 
     barrier = pltpu.get_barrier_semaphore()
-    for side in (LEFT, RIGHT):
-        @pl.when(has[side])
+    beside = pairs
+    for other in (t - 1, t + 1, t - 2, t + 2):
+        there = (other >= 0) & (other < owners)
+        beside += jnp.where(there, 1, 0)
+
+        @pl.when(there)
         def _():
             pl.semaphore_signal(
-                barrier, inc=1, device_id=towards[side], device_id_type=pl.DeviceIdType.MESH
+                barrier, inc=1, device_id={"tiles": other}, device_id_type=pl.DeviceIdType.MESH
             )
     pl.semaphore_signal(barrier, inc=1, device_id=sibling, device_id_type=pl.DeviceIdType.MESH)
     for d in range(1, pairs):
@@ -111,17 +120,16 @@
         held[order[i]] = block
         win[count + order[i]] = block
 
-    convert(0)
-    neighbours = jnp.where(has[LEFT], 1, 0) + jnp.where(has[RIGHT], 1, 0)
-    pl.semaphore_wait(barrier, pairs + neighbours)
-
-    for h, rows in enumerate(rows_of):
-        for side in (LEFT, RIGHT):
-            there = 1 - side
-            send(
-                held.at[r, rows], win.at[2 * count * there + r, rows],
-                wx_s.at[side, h], wx_r.at[there, h], towards[side], has[side],
-            )
+    for i in range(pairs):
+        convert(i)
+    pl.semaphore_wait(barrier, beside)
+
+    pieces = [(q, h) for q in range(pairs) for h in range(CHUNKS)]
+    for q, h in pieces:
+        send(
+            held.at[2 * q + c, rows_of[h]], win.at[far_base + 2 * q + c, rows_of[h]],
+            wx_s.at[q, h], wx_r.at[q, h], {"tiles": near},
+        )
     for side in (LEFT, RIGHT):
         @pl.when(jnp.logical_not(has[side]))
         def _():
@@ -130,7 +138,7 @@
             )
             r3[side] = jnp.zeros((keypoints, universe), jnp.bfloat16)
 
-    for i in range(1, count):
+    for i in range(pairs, count):
         convert(i)
 
     first = [pairs_ref[k, 0] - t * count for k in range(tiles)]
@@ -180,72 +188,56 @@
             total += r2[side, h, d - 1].astype(jnp.float32)
         return total
 
-    def window_slot(side, m, rows):
-        return win.at[2 * count * side + m, rows]
-
-    def window_out(h):
-        rows = rows_of[h]
-        for side in (LEFT, RIGHT):
-            mine = window_slot(side, r, rows)
-
-            @pl.when(has[side])
-            def _():
-                arrived(mine, wx_s.at[side, h], wx_r.at[side, h], towards[side])
-
-            for d in range(1, pairs):
-                send(
-                    mine, mine, wy_s.at[side, h, d - 1], wy_r.at[side, h, d - 1],
-                    across(d), has[side],
-                )
-            send(mine, mine, wc_s.at[side, h, 0], wc_r.at[side, h, 0], sibling, has[side])
-
-    def window_pass(h):
-        rows = rows_of[h]
-        for side in (LEFT, RIGHT):
-            for d in range(1, pairs):
-                q = lax.rem(p - d + pairs, pairs)
-                theirs = window_slot(side, 2 * q + c, rows)
-
-                @pl.when(has[side])
-                def _():
-                    arrived(
-                        theirs, wy_s.at[side, h, d - 1], wy_r.at[side, h, d - 1], across(d)
-                    )
-
-                send(
-                    theirs, theirs, wc_s.at[side, h, d], wc_r.at[side, h, d], sibling, has[side]
-                )
-
-    def window_end(h):
-        rows = rows_of[h]
-        for side in (LEFT, RIGHT):
-            for d in range(pairs):
-                q = lax.rem(p - d + pairs, pairs)
-
-                @pl.when(has[side])
-                def _():
-                    arrived(
-                        window_slot(side, 2 * q + (1 - c), rows),
-                        wc_s.at[side, h, d], wc_r.at[side, h, d], sibling,
-                    )
+    def window_near(q, h):
+        m, rows = 2 * q + c, rows_of[h]
+        slot = win.at[near_base + m, rows]
+        arrived(slot, wx_s.at[q, h], wx_r.at[q, h], {"tiles": near})
+        send(
+            slot, win.at[far_base + m, rows], wy_s.at[q, h], wy_r.at[q, h],
+            {"tiles": t + onward}, passes,
+        )
+        send(slot, slot, wc_s.at[0, q, h], wc_r.at[0, q, h], sibling)
+
+    def window_far(q, h):
+        slot = win.at[far_base + 2 * q + c, rows_of[h]]
+
+        @pl.when(fed)
+        def _():
+            arrived(slot, wy_s.at[q, h], wy_r.at[q, h], {"tiles": t - onward})
+
+        send(slot, slot, wc_s.at[1, q, h], wc_r.at[1, q, h], sibling, fed)
+
+    def window_end(q, h):
+        m, rows = 2 * q + (1 - c), rows_of[h]
+        arrived(win.at[near_base + m, rows], wc_s.at[0, q, h], wc_r.at[0, q, h], sibling)
+
+        @pl.when(fed)
+        def _():
+            arrived(win.at[far_base + m, rows], wc_s.at[1, q, h], wc_r.at[1, q, h], sibling)
 
     for h in range(CHUNKS):
         for side in (LEFT, RIGHT):
             pair_send(side, h)
+    split_at = len(pieces) // 2
     for h in range(CHUNKS):
-        window_out(h)
         for side in (LEFT, RIGHT):
             across_send(side, h)
+        if h < split_at:
+            window_near(*pieces[h])
+    for piece in pieces[min(CHUNKS, split_at):]:
+        window_near(*piece)
     for h in range(CHUNKS):
-        window_pass(h)
         for side in (LEFT, RIGHT):
             s3[side, rows_of[h]] = rep_sum(side, h).astype(jnp.bfloat16)
             send(
                 s3.at[side, rows_of[h]], r3.at[1 - side, rows_of[h]],
                 g3_s.at[side, h], g3_r.at[1 - side, h], towards[side], has[side],
             )
-    for h in range(CHUNKS):
-        window_end(h)
+        window_far(*pieces[h])
+    for piece in pieces[CHUNKS:]:
+        window_far(*piece)
+    for piece in pieces:
+        window_end(*piece)
 
     for h, rows in enumerate(rows_of):
         for k in range(tiles):
@@ -339,8 +331,8 @@
         ),
         in_specs=[
             pl.BlockSpec(memory_space=pltpu.SMEM),
-            pl.BlockSpec(memory_space=pl.ANY),
-            pl.BlockSpec(memory_space=pl.ANY),
+            pl.BlockSpec(memory_space=pltpu.HBM),
+            pl.BlockSpec(memory_space=pltpu.HBM),
         ],
         out_specs=(
             pl.BlockSpec(memory_space=pltpu.VMEM),
@@ -361,9 +353,9 @@
             pltpu.VMEM((2, *image), bf),
             pltpu.VMEM(image, f32),
             dma((count + tiles,)),
-            dma((2, C)), dma((2, C)),
-            dma((2, C, D)), dma((2, C, D)),
-            dma((2, C, pairs)), dma((2, C, pairs)),
+            dma((pairs, C)), dma((pairs, C)),
+            dma((pairs, C)), dma((pairs, C)),
+            dma((2, pairs, C)), dma((2, pairs, C)),
             dma((3, C)), dma((3, C)),
             dma((3, C, D)), dma((3, C, D)),
             dma((2, C)), dma((2, C)),

time: 64.3 us -> 49 us (0.76)
  Pallas kernels: 58.5 us -> 43 us
    pallas_call x1, Pallas kernels: 58.5 us -> 43 us  [shards(): pl.pallas_call(functools.partial(kernel, owners, rep), out_shape=(jax.Sha...]
where the time goes in v2:
time: 49 us; the launch traced here: 48.6 us
  Pallas kernels  43 us (88%)
  local copies, waits for them, and re-layouts  3.95 us (8%)
  other arithmetic  1.58 us (3%)
    pallas_call x1, Pallas kernels, shards(): pl.pallas_call(functools.partial(kernel, owners, rep), out_shape=(jax.Sha...  43 us
    unnamed x5, local copies, waits for them, and re-layouts  3.95 us
    select_n x1, other arithmetic, shards(): return jnp.where(mine, own[None], gathered.astype(f32))  1.58 us

profile of v2, /device:TPU:3, one launch (start us, length us, event | category | flops | bytes accessed | tf_op | source)
XLA Modules:
  0.0 48.6 jit_solution(1815568013603011248)
XLA Ops:
  0.0 0.8 %copy.4.pairs_ref = s32[4,2]{1,0:T(4,128)S(1)} copy(s32[4,2]{0,1:T(2,128)} %param.4) | data formatting | bytes 64 | tf_op args[1]
  0.8 0.0 copy-start
  0.8 1.6 %copy-done = bf16[4,512,512]{2,1,0:T(8,128)(2,1)S(1)} copy-done((bf16[4,512,512]{2,1,0:T(8,128)(2,1)S(1)}, bf16[4,512,512]{2,1,0:T(8,128)(2,1)}, u32[]{:S(2)}) %copy-start) | copy-done | bytes 2097176
  2.4 0.0 copy-start.1
  2.4 1.6 %copy-done.1 = f32[4,512,256]{2,1,0:T(8,128)S(1)} copy-done((f32[4,512,256]{2,1,0:T(8,128)S(1)}, f32[4,512,256]{2,1,0:T(8,128)}, u32[]{:S(2)}) %copy-start.1) | copy-done | bytes 2097176
  4.0 43.0 %shard_map.37 = (bf16[4,512,256]{2,1,0:T(8,128)(2,1)S(1)}, f32[512,256]{1,0:T(8,128)S(1)}) custom-call(s32[4,2]{1,0:T(4,128)S(1)} %copy.4.pairs_ref, bf16[4,512,512]{2,1,0:T(8,128)(2,1)S(1)} %copy-done, f32[4,512,256]{2,1,0:T(8,128)S(1)} %copy-done.1), custom_call_target="tpu_custom_call" | custom-call | tf_op jit(solution)/shard_map/pallas_call | solution.py:326
  47.0 1.6 %convert_select_fusion = f32[4,512,256]{2,1,0:T(8,128)} fusion(bf16[4,512,256]{2,1,0:T(8,128)(2,1)S(1)} %get-tuple-element.8, f32[512,256]{1,0:T(8,128)S(1)} %get-tuple-element.7, pred[4]{0:T(512)(128)(4,1)S(1)} %iota_compare_fusion), kind=kLoop, calls=%fused_computation | loop fusion | flops 1048576 | bytes 3670020 | tf_op jit(solution)/shard_map/jit(_where)/select_n | solution.py:370
  (1 shorter events, 0.0 us)
Async XLA Ops:
  0.8 1.6 %copy-start = (bf16[4,512,512]{2,1,0:T(8,128)(2,1)S(1)}, bf16[4,512,512]{2,1,0:T(8,128)(2,1)}, u32[]{:S(2)}) copy-start(bf16[4,512,512]{2,1,0:T(8,128)(2,1)} %aff_hbm.1) | copy-start | bytes 6291460
  2.4 1.6 %copy-start.1 = (f32[4,512,256]{2,1,0:T(8,128)S(1)}, f32[4,512,256]{2,1,0:T(8,128)}, u32[]{:S(2)}) copy-start(f32[4,512,256]{2,1,0:T(8,128)} %fac_hbm.1) | copy-start | bytes 6291460

commit v3 on v2

--- a/solution.py
+++ b/solution.py
@@ -145,7 +145,12 @@
     second = [pairs_ref[k, 1] - (t - 1) * count for k in range(tiles)]
     for k in range(tiles):
         aff_loads[k].wait()
-        back[k] = dot_t(aff[k], held[jnp.clip(first[k], 0, count - 1)])
+
+    def backward(h):
+        for k in range(tiles):
+            back[k, rows_of[h]] = dot_t(
+                aff[k, :, rows_of[h]], held[jnp.clip(first[k], 0, count - 1)]
+            )
 
     def partial(side, m, rows):
         slot = (0, 2 * count, count)[side] + m
@@ -215,11 +220,13 @@
         def _():
             arrived(win.at[far_base + m, rows], wc_s.at[1, q, h], wc_r.at[1, q, h], sibling)
 
+    split_at = len(pieces) // 2
+    backward(0)
     for h in range(CHUNKS):
         for side in (LEFT, RIGHT):
             pair_send(side, h)
-    split_at = len(pieces) // 2
-    for h in range(CHUNKS):
+        if h + 1 < CHUNKS:
+            backward(h + 1)
         for side in (LEFT, RIGHT):
             across_send(side, h)
         if h < split_at:

time: 49 us -> 48.8 us (level)
  no operation moved by 1% of the time
where the time goes in v3:
time: 48.8 us; the launch traced here: 48.6 us
  Pallas kernels  43 us (88%)
  local copies, waits for them, and re-layouts  3.95 us (8%)
  other arithmetic  1.58 us (3%)
    pallas_call x1, Pallas kernels, shards(): pl.pallas_call(functools.partial(kernel, owners, rep), out_shape=(jax.Sha...  43 us
    unnamed x5, local copies, waits for them, and re-layouts  3.95 us
    select_n x1, other arithmetic, shards(): return jnp.where(mine, own[None], gathered.astype(f32))  1.58 us

profile of v3, /device:TPU:3, one launch (start us, length us, event | category | flops | bytes accessed | tf_op | source)
XLA Modules:
  0.0 48.6 jit_solution(15193048978710153932)
XLA Ops:
  0.0 0.8 %copy.4.pairs_ref = s32[4,2]{1,0:T(4,128)S(1)} copy(s32[4,2]{0,1:T(2,128)} %param.4) | data formatting | bytes 64 | tf_op args[1]
  0.8 0.0 copy-start
  0.8 1.6 %copy-done = bf16[4,512,512]{2,1,0:T(8,128)(2,1)S(1)} copy-done((bf16[4,512,512]{2,1,0:T(8,128)(2,1)S(1)}, bf16[4,512,512]{2,1,0:T(8,128)(2,1)}, u32[]{:S(2)}) %copy-start) | copy-done | bytes 2097176
  2.4 0.0 copy-start.1
  2.4 1.6 %copy-done.1 = f32[4,512,256]{2,1,0:T(8,128)S(1)} copy-done((f32[4,512,256]{2,1,0:T(8,128)S(1)}, f32[4,512,256]{2,1,0:T(8,128)}, u32[]{:S(2)}) %copy-start.1) | copy-done | bytes 2097176
  4.0 43.0 %shard_map.37 = (bf16[4,512,256]{2,1,0:T(8,128)(2,1)S(1)}, f32[512,256]{1,0:T(8,128)S(1)}) custom-call(s32[4,2]{1,0:T(4,128)S(1)} %copy.4.pairs_ref, bf16[4,512,512]{2,1,0:T(8,128)(2,1)S(1)} %copy-done, f32[4,512,256]{2,1,0:T(8,128)S(1)} %copy-done.1), custom_call_target="tpu_custom_call" | custom-call | tf_op jit(solution)/shard_map/pallas_call | solution.py:333
  47.0 1.6 %convert_select_fusion = f32[4,512,256]{2,1,0:T(8,128)} fusion(bf16[4,512,256]{2,1,0:T(8,128)(2,1)S(1)} %get-tuple-element.8, f32[512,256]{1,0:T(8,128)S(1)} %get-tuple-element.7, pred[4]{0:T(512)(128)(4,1)S(1)} %iota_compare_fusion), kind=kLoop, calls=%fused_computation | loop fusion | flops 1048576 | bytes 3670020 | tf_op jit(solution)/shard_map/jit(_where)/select_n | solution.py:377
  (1 shorter events, 0.0 us)
Async XLA Ops:
  0.8 1.6 %copy-start = (bf16[4,512,512]{2,1,0:T(8,128)(2,1)S(1)}, bf16[4,512,512]{2,1,0:T(8,128)(2,1)}, u32[]{:S(2)}) copy-start(bf16[4,512,512]{2,1,0:T(8,128)(2,1)} %aff_hbm.1) | copy-start | bytes 6291460
  2.4 1.6 %copy-start.1 = (f32[4,512,256]{2,1,0:T(8,128)S(1)}, f32[4,512,256]{2,1,0:T(8,128)}, u32[]{:S(2)}) copy-start(f32[4,512,256]{2,1,0:T(8,128)} %fac_hbm.1) | copy-start | bytes 6291460
